TPU v7x, 32 devices: a whole 2x2x4 slice. The times are simulated.
32 devices in a mesh: expert: 16 (over z, y, x), tp: 2 (over core).
Axes of the slice: x: 2, y: 2, z: 4, core: 2. Of those that a mesh axis runs over, the one named last changes fastest.
Arguments:
- tokens: bfloat16 [1024, 2880], P(('expert', 'tp')), may hold values from -6 to 6
- expert_ids: int32 [1024, 4], P(('expert', 'tp')), may hold values from 0 to 15, all different within a row; in each aligned block of 32 rows (0 to 31, 32 to 63, ...) at most 16 rows name the same one
- route_logits: float32 [1024, 4], P(('expert', 'tp')), may hold values from -4 to 4
- gate_weight: bfloat16 [16, 2880, 1440], P('expert', None, 'tp'), may hold values from -0.109375 to 0.109375
- up_weight: bfloat16 [16, 2880, 1440], P('expert', None, 'tp'), may hold values from -0.109375 to 0.109375
- down_weight: bfloat16 [16, 1440, 2880], P('expert', 'tp'), may hold values from -0.15625 to 0.15625
Outputs:
- mixed_out: bfloat16 [1024, 2880], P(('expert', 'tp'))
Inputs may be any that keep to these rules, and one draw needn't show every extreme that they name: `expert_ids`: within each aligned block of 32 tokens (the tokens of one device) every token names 4 different experts and no expert is named more than 16 times; in every draw some expert is named exactly 16 times in some block.
All inputs are finite; a program needn't handle non-finite values.
Results may differ from a plain program's by a relative error of at most 0.0058.
Values may be sent and summed in bfloat16 or wider, within the bound.
A program may use at most 128 MiB of HBM per device.

v0:
```python
import jax
import jax.numpy as jnp
from jax import lax
from jax.sharding import PartitionSpec as P


def body(tokens, expert_ids, route_logits, gate_weight, up_weight, down_weight):
    experts = lax.axis_size("expert")
    tok_dev, model_width = tokens.shape
    pick_count = expert_ids.shape[1]
    capacity = 2 * tok_dev * pick_count // experts
    flat_ids = expert_ids.reshape(-1)
    one_hot = (flat_ids[:, None] == jnp.arange(experts, dtype=jnp.int32)[None, :]).astype(jnp.int32)
    earlier = jnp.cumsum(one_hot, axis=0) - one_hot
    slot_index = jnp.sum(earlier * one_hot, axis=1)
    position = flat_ids * capacity + slot_index
    slot_range = jnp.arange(experts * capacity, dtype=jnp.int32)
    matches = (position[:, None] == slot_range[None, :]).astype(jnp.int32)
    placing = jnp.sum(matches.reshape(tok_dev, pick_count, -1), axis=1).astype(jnp.bfloat16)
    outgoing = lax.dot_general(
        placing, tokens, (((0,), (0,)), ((), ())), preferred_element_type=jnp.float32
    )
    outgoing = outgoing.astype(jnp.bfloat16).reshape(experts, capacity, model_width)
    gate_local = gate_weight[0]
    up_local = up_weight[0]
    down_local = down_weight[0]
    received = lax.all_to_all(outgoing, "expert", split_axis=0, concat_axis=0, tiled=True)
    items = received.shape[1]
    row_total = experts * items
    row_block = received.reshape(row_total, model_width)
    paired = lax.all_gather(row_block, "tp", axis=0, tiled=True)
    gate_act = jnp.dot(paired, gate_local, preferred_element_type=jnp.float32)
    up_act = jnp.dot(paired, up_local, preferred_element_type=jnp.float32)
    hidden = (gate_act * jax.nn.sigmoid(1.702 * gate_act) * (up_act + 1.0)).astype(jnp.bfloat16)
    summed = lax.psum_scatter(
        jnp.dot(hidden, down_local, preferred_element_type=jnp.float32),
        "tp",
        scatter_dimension=0,
        tiled=True,
    )
    results = summed.astype(jnp.bfloat16).reshape(experts, items, model_width)
    returned = lax.all_to_all(results, "expert", split_axis=0, concat_axis=0, tiled=True).reshape(
        experts * capacity, model_width
    )
    picked = returned[position.reshape(tok_dev, pick_count)]
    scores = jnp.exp(route_logits)
    weights = scores / jnp.sum(scores, axis=1, keepdims=True)
    mixed_out = jnp.sum(weights[:, :, None] * picked.astype(jnp.float32), axis=1)
    return mixed_out.astype(jnp.bfloat16)


def solution(mesh):
    placed = (
        P(("expert", "tp"), None),
        P(("expert", "tp"), None),
        P(("expert", "tp"), None),
        P("expert", None, "tp"),
        P("expert", None, "tp"),
        P("expert", "tp", None),
    )
    return jax.shard_map(
        body, mesh=mesh, in_specs=placed, out_specs=P(("expert", "tp"), None), check_vma=False
    )
```

profile of v0, /device:TPU:0, one launch (start us, length us, event | category | flops | bytes accessed | tf_op | source)
XLA Modules:
  0.0 152.7 jit_solution(9339659452258564377)
XLA Ops:
  6.5 0.8 copy.26
  7.3 0.1 eq.29
  7.4 0.1 fusion.10
  7.5 0.2 reduce_window_sum.11
  7.7 0.2 select_reduce_fusion
  7.9 0.1 reduce_sum.40
  8.1 0.7 compare_select_fusion
  8.9 0.6 convolution_convert_fusion
  9.5 1.0 copy.28
  10.5 44.6 %all_to_all.10 = bf16[16,16,2880]{2,1,0:T(8,128)(2,1)} all-to-all(bf16[16,16,2880]{2,1,0:T(8,128)(2,1)S(1)} %bitcast.22), channel_id=1, replica_groups=mesh['expert'=16,'tp'=2] {'expert'}, dimensions={0} | all-to-all | bytes 2949120 | tf_op jit(solution)/shard_map/all_to_all | solution.py:27
  55.1 10.2 %all-gather.2.cloned.1.call-done = bf16[512,2880]{1,0:T(8,128)(2,1)} async-done(((bf16[256,2880]{1,0:T(8,128)(2,1)}), bf16[512,2880]{1,0:T(8,128)(2,1)}) %all-gather.2.cloned.1.call-update) | async-done | bytes 2949136 | tf_op jit(solution)/shard_map/all_gather | solution.py:31
  65.3 6.9 %fusion.4 = f32[512,720]{0,1:T(8,128)} fusion(bf16[512,2880]{1,0:T(8,128)(2,1)} %all-gather.2.cloned.1.call-done, bf16[1,2880,720]{1,2,0:T(8,128)(2,1)} %param.9), kind=kOutput, calls=%fused_computation.5 | convolution fusion | flops 2123366400 | bytes 8570880 | tf_op jit(solution)/shard_map/dot_general | solution.py:32
  72.2 11.4 %fusion = f32[512,2880]{0,1:T(8,128)} fusion(bf16[1,720,2880]{2,1,0:T(8,128)(2,1)} %param.11, f32[512,720]{0,1:T(8,128)} %fusion.4, bf16[512,2880]{1,0:T(8,128)(2,1)S(1)} %copy-done.2, bf16[1,2880,720]{1,2,0:T(8,128)(2,1)} %param.10), kind=kOutput, calls=%fused_computation.1 | convolution fusion | flops 4249681920 | bytes 18616320 | tf_op jit(solution)/shard_map/dot_general | solution.py:36
  83.6 15.3 %reduce-scatter.2.cloned.1.call-done = f32[256,2880]{0,1:T(8,128)} async-done(((f32[512,2880]{0,1:T(8,128)}), f32[256,2880]{0,1:T(8,128)}) %reduce-scatter.2.cloned.1.call-update) | async-done | bytes 2949136 | tf_op jit(solution)/shard_map/reduce_scatter | solution.py:35
  98.8 2.0 %convert_element_type.30 = bf16[256,2880]{0,1:T(8,128)(2,1)S(1)} convert(f32[256,2880]{0,1:T(8,128)} %reduce-scatter.2.cloned.1.call-done) | non-fusion elementwise | flops 737280 | bytes 4423680 | tf_op jit(solution)/shard_map/convert_element_type | solution.py:41
  100.8 1.7 %copy.29 = bf16[256,2880]{1,0:T(8,128)(2,1)} copy(bf16[256,2880]{0,1:T(8,128)(2,1)S(1)} %convert_element_type.30) | data formatting | bytes 2949120 | tf_op jit(solution)/shard_map/convert_element_type | solution.py:41
  102.6 7.0 %all-to-all-start.1 = ((bf16[16,16,2880]{2,1,0:T(8,128)(2,1)}), bf16[16,16,2880]{2,1,0:T(8,128)(2,1)S(1)}, u32[]{:S(2)}, u32[]{:S(2)}) async-start(bf16[16,16,2880]{2,1,0:T(8,128)(2,1)} %bitcast.5), calls=%async_computation.2 | async-start | bytes 3014656 | tf_op jit(solution)/shard_map/all_to_all | solution.py:42
  109.5 0.1 copy.30
  109.6 0.1 reshape.41
  109.8 0.1 copy.25
  109.9 32.8 %all-to-all-done.1 = bf16[16,16,2880]{2,1,0:T(8,128)(2,1)S(1)} async-done(((bf16[16,16,2880]{2,1,0:T(8,128)(2,1)}), bf16[16,16,2880]{2,1,0:T(8,128)(2,1)S(1)}, u32[]{:S(2)}, u32[]{:S(2)}) %all-to-all-start.1) | async-done | bytes 1474592 | tf_op jit(solution)/shard_map/all_to_all | solution.py:42
  142.7 1.1 gather_fusion
  143.7 0.4 reshape.49
  144.1 1.7 %multiply_reduce_fusion = bf16[32,2880]{1,0:T(8,128)(2,1)} fusion(f32[32,4,2880]{2,1,0:T(4,128)S(1)} %reshape.49, f32[32,4]{1,0:T(8,128)S(1)} %copy.25), kind=kLoop, calls=%fused_computation.8 | loop fusion | flops 645120 | bytes 1659392 | tf_op jit(solution)/shard_map/reduce_sum | solution.py:48
  (15 shorter events, 0.3 us)
Async XLA Ops:
  6.5 2.3 %copy-start = (bf16[32,2880]{1,0:T(8,128)(2,1)S(1)}, bf16[32,2880]{1,0:T(8,128)(2,1)}, u32[]{:S(2)}) copy-start(bf16[32,2880]{1,0:T(8,128)(2,1)} %param.6) | copy-start | bytes 552964
  6.5 58.7 %all-gather.2.cloned.1.call-start = ((), (), s32[]{:S(2)}) async-start(), calls=%async_computation.3 | async-start | bytes 4521984 | tf_op jit(solution)/shard_map/all_gather | solution.py:31
  55.1 43.8 %reduce-scatter.2.cloned.1.call-start = ((), (), s32[]{:S(2)}) async-start(), calls=%async_computation.4 | async-start | bytes 8847360 | tf_op jit(solution)/shard_map/reduce_scatter | solution.py:35
  65.3 6.9 %copy-start.2 = (bf16[512,2880]{1,0:T(8,128)(2,1)S(1)}, bf16[512,2880]{1,0:T(8,128)(2,1)}, u32[]{:S(2)}) copy-start(bf16[512,2880]{1,0:T(8,128)(2,1)} %all-gather.2.cloned.1.call-done) | copy-start | bytes 8847364
  102.5 7.2 %copy-start.1 = (f32[32,4]{0,1:T(4,128)S(1)}, f32[32,4]{0,1:T(4,128)}, u32[]{:S(2)}) copy-start(f32[32,4]{0,1:T(4,128)} %param.8) | copy-start | bytes 1540
  102.6 40.1 %all-to-all-start.1 = ((bf16[16,16,2880]{2,1,0:T(8,128)(2,1)}), bf16[16,16,2880]{2,1,0:T(8,128)(2,1)S(1)}, u32[]{:S(2)}, u32[]{:S(2)}) async-start(bf16[16,16,2880]{2,1,0:T(8,128)(2,1)} %bitcast.5), calls=%async_computation.2 | async-start | bytes 3014656 | tf_op jit(solution)/shard_map/all_to_all | solution.py:42
Sparse Core Ops, SparseCore 0:
  55.2 10.0 all-gather.1
  83.7 15.1 reduce-scatter.1
where the time goes:
time: 155 us; the launch traced here: 153 us
  waiting for transfers between devices  58.3 us (38%)
  blocking collectives  44.6 us (29%)
  matrix products  18.8 us (12%)
  between operations  13.5 us (9%)
  starting transfers between devices  7.02 us (5%)
  local copies, waits for them, and re-layouts  5.5 us (4%)
  other arithmetic  4.93 us (3%)
    all_to_all x1, blocking collectives, body(): lax.all_to_all(outgoing, 'expert', split_axis=0, concat_axis=0, tiled=True)  44.6 us
    all_to_all x1, waiting for transfers between devices, body(): lax.all_to_all(results, 'expert', split_axis=0, concat_axis=0, tiled=True)  32.8 us
    reduce_scatter x1, waiting for transfers between devices, body(): lax.psum_scatter(jnp.dot(hidden, down_local, preferred_element_type=jnp.f...  15.3 us
    dot_general x1, matrix products, body(): jnp.dot(hidden, down_local, preferred_element_type=jnp.float32)  11.4 us
    all_gather x1, waiting for transfers between devices, body(): paired = lax.all_gather(row_block, 'tp', axis=0, tiled=True)  10.2 us
    all_to_all x1, starting transfers between devices, body(): lax.all_to_all(results, 'expert', split_axis=0, concat_axis=0, tiled=True)  6.97 us
    dot_general x1, matrix products, body(): gate_act = jnp.dot(paired, gate_local, preferred_element_type=jnp.float32)  6.88 us
  transfers between devices with their start and end apart: 3, of which 3 were waited for; matrix products, arithmetic and copies ran while one was open for 0% of the time, Pallas kernels for 0%

commit v1 on v0

--- a/solution.py
+++ b/solution.py
@@ -1,18 +1,313 @@
+import functools
+
 import jax
 import jax.numpy as jnp
 from jax import lax
+from jax.experimental import pallas as pl
+from jax.experimental.pallas import tpu as pltpu
 from jax.sharding import PartitionSpec as P
 
-
-def body(tokens, expert_ids, route_logits, gate_weight, up_weight, down_weight):
+MESH = pl.DeviceIdType.MESH
+F32 = jnp.float32
+BF16 = jnp.bfloat16
+
+
+def flip(a, b, extent):
+    total, bit = 0, 1
+    while bit < extent:
+        total = total + ((a // bit + b // bit) % 2) * bit
+        bit *= 2
+    return total
+
+
+def moe_kernel(
+    sizes,
+    tok_ref, ids_ref, logit_ref, gate_hbm, up_hbm, down_hbm,
+    out_ref,
+    zbuf, xs, xr, gate_w, up_w, down_w, part, tbuf, trecv, ybuf, yrecv, cbuf, crecv, acc,
+    wsem, zsend_sem, zrecv_sem, xsend_sem, xrecv_sem, fsend_sem, frecv_sem,
+    tsend_sem, trecv_sem, ysend_sem, yrecv_sem, csend_sem, crecv_sem,
+):
+    outer, inner, cap, picks, width, wide = sizes
+    tok_count = tok_ref.shape[0]
+    group = inner * cap
+    e, c = lax.axis_index("expert"), lax.axis_index("tp")
+    z, p = e // inner, e % inner
+    other = 1 - c
+
+    loads = [
+        pltpu.make_async_copy(gate_hbm.at[0], gate_w.at[pl.ds(0, width)], wsem.at[0]),
+        pltpu.make_async_copy(up_hbm.at[0], up_w.at[pl.ds(0, width)], wsem.at[1]),
+        pltpu.make_async_copy(down_hbm.at[0], down_w, wsem.at[2]),
+    ]
+    for load in loads:
+        load.start()
+
+    barrier = pltpu.get_barrier_semaphore()
+    for d in range(1, outer):
+        pl.semaphore_signal(barrier, inc=1, device_id=(flip(z, d, outer) * inner + p, c), device_id_type=MESH)
+    for d in range(1, inner):
+        pl.semaphore_signal(barrier, inc=1, device_id=(z * inner + flip(p, d, inner), c), device_id_type=MESH)
+    pl.semaphore_signal(barrier, inc=1, device_id=(e, other), device_id_type=MESH)
+
+    experts = outer * inner
+    ids = ids_ref[...]
+    expert_lane = lax.broadcasted_iota(jnp.int32, (tok_count, experts), 1)
+    named = [(ids[:, k : k + 1] == expert_lane).astype(F32) for k in range(picks)]
+    lower = (
+        lax.broadcasted_iota(jnp.int32, (tok_count, tok_count), 1)
+        < lax.broadcasted_iota(jnp.int32, (tok_count, tok_count), 0)
+    ).astype(F32)
+    earlier = jnp.dot(lower, sum(named), preferred_element_type=F32)
+    scores = jnp.exp(logit_ref[...])
+    weights = scores / jnp.sum(scores, axis=1, keepdims=True)
+    tail = tok_ref[:, wide - 128 :].astype(F32)
+    lane = lax.broadcasted_iota(jnp.int32, (tok_count, 128), 1)
+    first = 128 - 4 * picks
+    for k in range(picks):
+        slot = jnp.sum(earlier * named[k], axis=1, keepdims=True)
+        weight = weights[:, k : k + 1]
+        high = weight.astype(BF16).astype(F32)
+        for j, value in enumerate((ids[:, k : k + 1].astype(F32), slot, high, weight - high)):
+            tail = jnp.where(lane == first + 4 * k + j, value, tail)
+    zbuf[0, :, : wide - 128] = tok_ref[:, : wide - 128]
+    zbuf[0, :, wide - 128 :] = tail.astype(BF16)
+    gate_w[width:, :] = jnp.zeros((wide - width, gate_w.shape[1]), BF16)
+    up_w[width:, :] = jnp.zeros((wide - width, up_w.shape[1]), BF16)
+
+    pl.semaphore_wait(barrier, outer + inner - 1)
+
+    def z_copy(s):
+        return pltpu.make_async_remote_copy(
+            src_ref=zbuf.at[0], dst_ref=zbuf.at[s], send_sem=zsend_sem.at[s], recv_sem=zrecv_sem.at[s],
+            device_id=(flip(z, s, outer) * inner + p, c), device_id_type=MESH,
+        )
+
+    def x_copy(s, d, receive=False):
+        peer = flip(p, d, inner)
+        return pltpu.make_async_remote_copy(
+            src_ref=xs.at[s, peer], dst_ref=xr.at[s, c, peer if receive else p],
+            send_sem=xsend_sem.at[s, d], recv_sem=xrecv_sem.at[s, d],
+            device_id=(z * inner + peer, c), device_id_type=MESH,
+        )
+
+    def f_copy(s, d, receive=False):
+        peer = flip(p, d, inner)
+        return pltpu.make_async_remote_copy(
+            src_ref=xr.at[s, c, peer], dst_ref=xr.at[s, other if receive else c, peer],
+            send_sem=fsend_sem.at[s, d], recv_sem=frecv_sem.at[s, d],
+            device_id=(e, other), device_id_type=MESH,
+        )
+
+    def t_copy(s):
+        return pltpu.make_async_remote_copy(
+            src_ref=tbuf.at[s], dst_ref=trecv.at[s], send_sem=tsend_sem.at[s], recv_sem=trecv_sem.at[s],
+            device_id=(e, other), device_id_type=MESH,
+        )
+
+    def y_copy(s, d, receive=False):
+        peer = flip(p, d, inner)
+        return pltpu.make_async_remote_copy(
+            src_ref=ybuf.at[s, peer], dst_ref=yrecv.at[s, peer if receive else p],
+            send_sem=ysend_sem.at[s, d], recv_sem=yrecv_sem.at[s, d],
+            device_id=(z * inner + peer, c), device_id_type=MESH,
+        )
+
+    def c_copy(s):
+        return pltpu.make_async_remote_copy(
+            src_ref=cbuf.at[s], dst_ref=crecv.at[s], send_sem=csend_sem.at[s], recv_sem=crecv_sem.at[s],
+            device_id=(flip(z, s, outer) * inner + p, c), device_id_type=MESH,
+        )
+
+    def notes(s):
+        told = zbuf[s, :, wide - 128 :].astype(F32)
+        found = []
+        for k in range(picks):
+            at = first + 4 * k
+            row = told[:, at : at + 1] * cap + told[:, at + 1 : at + 2] - (z * group).astype(F32)
+            found.append((row, told[:, at + 2 : at + 3], told[:, at + 3 : at + 4]))
+        return found
+
+    def slots():
+        return lax.broadcasted_iota(jnp.int32, (tok_count, group), 1).astype(F32)
+
+    def dispatch(s):
+        rows = slots()
+        placing = sum((row == rows).astype(F32) for row, _, _ in notes(s)).astype(BF16)
+        packed = lax.dot_general(placing, zbuf[s], (((0,), (0,)), ((), ())), preferred_element_type=F32)
+        xs[s] = packed.astype(BF16).reshape(inner, cap, wide)
+        for d in range(1, inner):
+            x_copy(s, d).start()
+        xr[s, c, p] = xs[s, p]
+        f_copy(s, 0).start()
+
+    def compute(s):
+        rows = xr[s].reshape(2 * group, wide)
+        gate_act = jnp.dot(rows, gate_w[...], preferred_element_type=F32)
+        up_act = jnp.dot(rows, up_w[...], preferred_element_type=F32)
+        hidden = (gate_act * jax.nn.sigmoid(1.702 * gate_act) * (up_act + 1.0)).astype(BF16)
+        part[s % 2] = jnp.dot(hidden, down_w[...], preferred_element_type=F32).reshape(2, group, width)
+        tbuf[s] = part[s % 2, other].astype(BF16)
+        t_copy(s).start()
+
+    def give_back(s):
+        t_copy(s).wait_recv()
+        whole = part[s % 2, c] + trecv[s].astype(F32)
+        ybuf[s] = whole.astype(BF16).reshape(inner, cap, width)
+        for d in range(1, inner):
+            y_copy(s, d).start()
+        yrecv[s, p] = ybuf[s, p]
+
+    def combine(s):
+        for d in range(1, inner):
+            y_copy(s, d, True).wait_recv()
+        rows = slots()
+        high = jnp.zeros((tok_count, group), F32)
+        low = jnp.zeros((tok_count, group), F32)
+        for row, weight_high, weight_low in notes(s):
+            high = high + jnp.where(row == rows, weight_high, 0.0)
+            low = low + jnp.where(row == rows, weight_low, 0.0)
+        mixing = jnp.concatenate([high, low], axis=0).astype(BF16)
+        both = jnp.dot(mixing, yrecv[s].reshape(group, width), preferred_element_type=F32)
+        return both[:tok_count] + both[tok_count:]
+
+    for s in range(1, outer):
+        z_copy(s).start()
+    dispatch(0)
+    for load in loads:
+        load.wait()
+
+    def step(i, carry):
+        @pl.when(i + 1 < outer)
+        def _():
+            z_copy(i + 1).wait_recv()
+            dispatch(i + 1)
+
+        @pl.when(i < outer)
+        def _():
+            for d in range(1, inner):
+                x_copy(i, d, True).wait_recv()
+                f_copy(i, d).start()
+            for d in range(inner):
+                f_copy(i, d, True).wait_recv()
+            compute(i)
+
+        @pl.when((i >= 1) & (i <= outer))
+        def _():
+            give_back(i - 1)
+
+        @pl.when(i == 2)
+        def _():
+            acc[...] = combine(0)
+
+        @pl.when(i > 2)
+        def _():
+            cbuf[i - 2] = combine(i - 2).astype(BF16)
+            c_copy(i - 2).start()
+
+        return carry
+
+    lax.fori_loop(0, outer + 2, step, 0)
+
+    total = acc[...]
+    for s in range(1, outer):
+        c_copy(s).wait_recv()
+        total = total + crecv[s].astype(F32)
+    out_ref[...] = total.astype(BF16)
+
+    for s in range(outer):
+        for d in range(1, inner):
+            x_copy(s, d).wait_send()
+            y_copy(s, d).wait_send()
+        for d in range(inner):
+            f_copy(s, d).wait_send()
+        t_copy(s).wait_send()
+        if s > 0:
+            z_copy(s).wait_send()
+            c_copy(s).wait_send()
+
+
+def split_of(experts):
+    inner = 1
+    while 4 * inner * inner <= experts:
+        inner *= 2
+    return experts // inner, inner
+
+
+def fused_plan(mesh, tokens, expert_ids, gate_weight):
+    experts, cores = mesh.shape["expert"], mesh.shape["tp"]
+    tok_dev, width = tokens.shape
+    picks, half = expert_ids.shape[1], gate_weight.shape[2]
+    cap = 2 * tok_dev * picks // experts
+    outer, inner = split_of(experts)
+    wide = -(-(width + 4 * picks) // 128) * 128
+    if cores != 2 or outer * inner != experts or experts & (experts - 1) or experts > 256:
+        return None
+    if cap % 16 or tok_dev % 16 or tok_dev > 256 or width % 16 or half % 16:
+        return None
+    rows = outer * inner * cap
+    lanes = -(-half // 128) * 128
+    held = 2 * wide * (2 * lanes + half + 7 * rows + 3 * outer * tok_dev) + 16 * wide * inner * cap
+    if held > 44 * 2**20:
+        return None
+    return outer, inner, cap, picks, width, wide
+
+
+def fused(sizes, tokens, expert_ids, route_logits, gate_weight, up_weight, down_weight):
+    outer, inner, cap, picks, width, wide = sizes
+    tok_dev = tokens.shape[0]
+    half = gate_weight.shape[2]
+    group = inner * cap
+    padded = jnp.pad(tokens, ((0, 0), (0, wide - width)))
+    vmem, hbm = pl.BlockSpec(memory_space=pltpu.VMEM), pl.BlockSpec(memory_space=pl.ANY)
+    dma = pltpu.SemaphoreType.DMA
+    rows = 2 * outer * group
+    return pl.pallas_call(
+        functools.partial(moe_kernel, sizes),
+        out_shape=jax.ShapeDtypeStruct((tok_dev, width), BF16),
+        in_specs=[vmem, vmem, vmem, hbm, hbm, hbm],
+        out_specs=vmem,
+        scratch_shapes=[
+            pltpu.VMEM((outer, tok_dev, wide), BF16),
+            pltpu.VMEM((outer, inner, cap, wide), BF16),
+            pltpu.VMEM((outer, 2, inner, cap, wide), BF16),
+            pltpu.VMEM((wide, half), BF16),
+            pltpu.VMEM((wide, half), BF16),
+            pltpu.VMEM((half, width), BF16),
+            pltpu.VMEM((2, 2, group, width), F32),
+            pltpu.VMEM((outer, group, width), BF16),
+            pltpu.VMEM((outer, group, width), BF16),
+            pltpu.VMEM((outer, inner, cap, width), BF16),
+            pltpu.VMEM((outer, inner, cap, width), BF16),
+            pltpu.VMEM((outer, tok_dev, width), BF16),
+            pltpu.VMEM((outer, tok_dev, width), BF16),
+            pltpu.VMEM((tok_dev, width), F32),
+            dma((3,)),
+            dma((outer,)), dma((outer,)),
+            dma((outer, inner)), dma((outer, inner)),
+            dma((outer, inner)), dma((outer, inner)),
+            dma((outer,)), dma((outer,)),
+            dma((outer, inner)), dma((outer, inner)),
+            dma((outer,)), dma((outer,)),
+        ],
+        compiler_params=pltpu.CompilerParams(
+            collective_id=0, has_side_effects=True, vmem_limit_bytes=56 * 2**20
+        ),
+        cost_estimate=pl.CostEstimate(
+            flops=6 * rows * width * half, bytes_accessed=6 * width * half, transcendentals=rows * half
+        ),
+    )(padded, expert_ids, route_logits, gate_weight, up_weight, down_weight)
+
+
+def plain(tokens, expert_ids, route_logits, gate_weight, up_weight, down_weight):
     experts = lax.axis_size("expert")
     tok_dev, model_width = tokens.shape
     pick_count = expert_ids.shape[1]
     capacity = 2 * tok_dev * pick_count // experts
     flat_ids = expert_ids.reshape(-1)
-    one_hot = (flat_ids[:, None] == jnp.arange(experts, dtype=jnp.int32)[None, :]).astype(jnp.int32)
-    earlier = jnp.cumsum(one_hot, axis=0) - one_hot
-    slot_index = jnp.sum(earlier * one_hot, axis=1)
+    pick_range = jnp.arange(flat_ids.shape[0], dtype=jnp.int32)
+    same = (flat_ids[:, None] == flat_ids[None, :]) & (pick_range[None, :] < pick_range[:, None])
+    slot_index = jnp.sum(same.astype(jnp.int32), axis=1)
     position = flat_ids * capacity + slot_index
     slot_range = jnp.arange(experts * capacity, dtype=jnp.int32)
     matches = (position[:, None] == slot_range[None, :]).astype(jnp.int32)
@@ -50,6 +345,11 @@
 
 
 def solution(mesh):
+    def body(tokens, expert_ids, route_logits, gate_weight, up_weight, down_weight):
+        sizes = fused_plan(mesh, tokens, expert_ids, gate_weight)
+        run = plain if sizes is None else functools.partial(fused, sizes)
+        return run(tokens, expert_ids, route_logits, gate_weight, up_weight, down_weight)
+
     placed = (
         P(("expert", "tp"), None),
         P(("expert", "tp"), None),

time: 155 us -> 80.1 us (0.52)
  the two profiles are of different devices: /device:TPU:0 before, /device:TPU:8 now
where the time goes in v1:
time: 80.1 us; the launch traced here: 79.6 us
  Pallas kernels  60.7 us (76%)
  local copies, waits for them, and re-layouts  19 us (24%)
    pallas_call x1, Pallas kernels, fused(): pl.pallas_call(functools.partial(moe_kernel, sizes), out_shape=jax.ShapeD...  60.7 us
    unnamed x5, local copies, waits for them, and re-layouts  17.3 us
    pad x1, local copies, waits for them, and re-layouts, fused(): padded = jnp.pad(tokens, ((0, 0), (0, wide - width)))  1.61 us

profile of v1, /device:TPU:8, one launch (start us, length us, event | category | flops | bytes accessed | tf_op | source)
XLA Modules:
  0.0 79.6 jit_solution(12426654137254380101)
XLA Ops:
  0.0 1.4 %copy.7.ids_ref = s32[32,4]{1,0:T(8,128)} copy(s32[32,4]{0,1:T(4,128)} %param.7) | data formatting | bytes 1024 | tf_op args[1]
  1.4 1.4 %copy.8.logit_ref = f32[32,4]{1,0:T(8,128)} copy(f32[32,4]{0,1:T(4,128)} %param.8) | data formatting | bytes 1024 | tf_op args[2]
  2.7 1.6 %pad.4.tok_ref = bf16[32,2944]{1,0:T(8,128)(2,1)} pad(bf16[32,2880]{1,0:T(8,128)(2,1)} %param.6, bf16[]{:T(256)} %constant.2.clone.1), padding=0_0x0_64 | pad | bytes 372738 | tf_op jit(solution)/shard_map/jit(_pad)/pad | solution.py:261
  4.3 6.5 %copy.9.gate_hbm = bf16[1,2880,720]{2,1,0:T(8,128)(2,1)} copy(bf16[1,2880,720]{1,2,0:T(8,128)(2,1)} %param.9) | data formatting | bytes 8294400 | tf_op args[3]
  10.8 6.5 %copy.10.up_hbm = bf16[1,2880,720]{2,1,0:T(8,128)(2,1)} copy(bf16[1,2880,720]{1,2,0:T(8,128)(2,1)} %param.10) | data formatting | bytes 8294400 | tf_op args[4]
  17.3 60.7 %shard_map.64 = bf16[32,2880]{1,0:T(8,128)(2,1)} custom-call(bf16[32,2944]{1,0:T(8,128)(2,1)} %pad.4.tok_ref, s32[32,4]{1,0:T(8,128)} %copy.7.ids_ref, f32[32,4]{1,0:T(8,128)} %copy.8.logit_ref, bf16[1,2880,720]{2,1,0:T(8,128)(2,1)} %copy.9.gate_hbm, bf16[1,2880,720]{2,1,0:T(8,128)(2,1)} %copy.10.up_hbm, bf16[1,720,2880]{2,1,0:T(8,128)(2,1)} %down_hbm.1), custom_call_target="tpu_custom_call" | custom-call | flops 6370099200 | bytes 12441600 | tf_op jit(solution)/shard_map/pallas_call | solution.py:265
  78.0 1.6 %copy.12 = bf16[32,2880]{1,0:T(8,128)(2,1)} copy(bf16[32,2880]{1,0:T(8,128)(2,1)} %shard_map.64) | data formatting | bytes 368640

commit v2 on v1

--- a/solution.py
+++ b/solution.py
@@ -36,8 +36,8 @@
     other = 1 - c
 
     loads = [
-        pltpu.make_async_copy(gate_hbm.at[0], gate_w.at[pl.ds(0, width)], wsem.at[0]),
-        pltpu.make_async_copy(up_hbm.at[0], up_w.at[pl.ds(0, width)], wsem.at[1]),
+        pltpu.make_async_copy(gate_hbm.at[0], gate_w, wsem.at[0]),
+        pltpu.make_async_copy(up_hbm.at[0], up_w, wsem.at[1]),
         pltpu.make_async_copy(down_hbm.at[0], down_w, wsem.at[2]),
     ]
     for load in loads:
@@ -45,43 +45,70 @@
 
     barrier = pltpu.get_barrier_semaphore()
     for d in range(1, outer):
-        pl.semaphore_signal(barrier, inc=1, device_id=(flip(z, d, outer) * inner + p, c), device_id_type=MESH)
+        pl.semaphore_signal(barrier, inc=1, device_id=((z + d) % outer * inner + p, c), device_id_type=MESH)
     for d in range(1, inner):
         pl.semaphore_signal(barrier, inc=1, device_id=(z * inner + flip(p, d, inner), c), device_id_type=MESH)
     pl.semaphore_signal(barrier, inc=1, device_id=(e, other), device_id_type=MESH)
 
     experts = outer * inner
-    ids = ids_ref[...]
     expert_lane = lax.broadcasted_iota(jnp.int32, (tok_count, experts), 1)
-    named = [(ids[:, k : k + 1] == expert_lane).astype(F32) for k in range(picks)]
-    lower = (
-        lax.broadcasted_iota(jnp.int32, (tok_count, tok_count), 1)
-        < lax.broadcasted_iota(jnp.int32, (tok_count, tok_count), 0)
-    ).astype(F32)
+    square = (tok_count, tok_count)
+    row_at, lane_at = lax.broadcasted_iota(jnp.int32, square, 0), lax.broadcasted_iota(jnp.int32, square, 1)
+
+    def upright(line):
+        return jnp.sum(jnp.where(row_at == lane_at, line, jnp.zeros_like(line)), axis=1, keepdims=True)
+
+    chosen = [upright(ids_ref[k : k + 1, :]) for k in range(picks)]
+    named = [(column == expert_lane).astype(F32) for column in chosen]
+    lower = (lane_at < row_at).astype(F32)
     earlier = jnp.dot(lower, sum(named), preferred_element_type=F32)
     scores = jnp.exp(logit_ref[...])
-    weights = scores / jnp.sum(scores, axis=1, keepdims=True)
-    tail = tok_ref[:, wide - 128 :].astype(F32)
+    weights = scores / jnp.sum(scores, axis=0, keepdims=True)
+    zbuf[z, :, wide - 128 :] = jnp.zeros((tok_count, 128), BF16)
+    zbuf[z, :, :width] = tok_ref[...]
+    tail = zbuf[z, :, wide - 128 :].astype(F32)
     lane = lax.broadcasted_iota(jnp.int32, (tok_count, 128), 1)
     first = 128 - 4 * picks
     for k in range(picks):
         slot = jnp.sum(earlier * named[k], axis=1, keepdims=True)
-        weight = weights[:, k : k + 1]
+        weight = upright(weights[k : k + 1, :])
         high = weight.astype(BF16).astype(F32)
-        for j, value in enumerate((ids[:, k : k + 1].astype(F32), slot, high, weight - high)):
+        for j, value in enumerate((chosen[k].astype(F32), slot, high, weight - high)):
             tail = jnp.where(lane == first + 4 * k + j, value, tail)
-    zbuf[0, :, : wide - 128] = tok_ref[:, : wide - 128]
-    zbuf[0, :, wide - 128 :] = tail.astype(BF16)
-    gate_w[width:, :] = jnp.zeros((wide - width, gate_w.shape[1]), BF16)
-    up_w[width:, :] = jnp.zeros((wide - width, up_w.shape[1]), BF16)
+    zbuf[z, :, wide - 128 :] = tail.astype(BF16)
 
     pl.semaphore_wait(barrier, outer + inner - 1)
 
-    def z_copy(s):
-        return pltpu.make_async_remote_copy(
-            src_ref=zbuf.at[0], dst_ref=zbuf.at[s], send_sem=zsend_sem.at[s], recv_sem=zrecv_sem.at[s],
-            device_id=(flip(z, s, outer) * inner + p, c), device_id_type=MESH,
-        )
+    def origin(s):
+        near = jnp.minimum(z, outer - 1 - z)
+        toward = jnp.where(2 * z < outer, -1, 1)
+        j = (s + 1) // 2
+        paired = jnp.where(s % 2 == 1, toward * j, -toward * j)
+        return z + jnp.where(s <= 2 * near, paired, -toward * (s - near))
+
+    def z_copy(block, way):
+        return pltpu.make_async_remote_copy(
+            src_ref=zbuf.at[block], dst_ref=zbuf.at[block],
+            send_sem=zsend_sem.at[way, block], recv_sem=zrecv_sem.at[block],
+            device_id=((z + 2 * way - 1) * inner + p, c), device_id_type=MESH,
+        )
+
+    def pass_on(d):
+        @pl.when(z >= d)
+        def _():
+            z_copy(z - d, 1).wait_recv()
+
+            @pl.when(z + 1 < outer)
+            def _():
+                z_copy(z - d, 1).start()
+
+        @pl.when(z + d < outer)
+        def _():
+            z_copy(z + d, 0).wait_recv()
+
+            @pl.when(z > 0)
+            def _():
+                z_copy(z + d, 0).start()
 
     def x_copy(s, d, receive=False):
         peer = flip(p, d, inner)
@@ -113,14 +140,15 @@
             device_id=(z * inner + peer, c), device_id_type=MESH,
         )
 
-    def c_copy(s):
-        return pltpu.make_async_remote_copy(
-            src_ref=cbuf.at[s], dst_ref=crecv.at[s], send_sem=csend_sem.at[s], recv_sem=crecv_sem.at[s],
-            device_id=(flip(z, s, outer) * inner + p, c), device_id_type=MESH,
+    def c_copy(s, peer, receive=False):
+        return pltpu.make_async_remote_copy(
+            src_ref=cbuf.at[s], dst_ref=crecv.at[peer if receive else z],
+            send_sem=csend_sem.at[s], recv_sem=crecv_sem.at[peer if receive else z],
+            device_id=(peer * inner + p, c), device_id_type=MESH,
         )
 
     def notes(s):
-        told = zbuf[s, :, wide - 128 :].astype(F32)
+        told = zbuf[origin(s), :, wide - 128 :].astype(F32)
         found = []
         for k in range(picks):
             at = first + 4 * k
@@ -134,7 +162,7 @@
     def dispatch(s):
         rows = slots()
         placing = sum((row == rows).astype(F32) for row, _, _ in notes(s)).astype(BF16)
-        packed = lax.dot_general(placing, zbuf[s], (((0,), (0,)), ((), ())), preferred_element_type=F32)
+        packed = lax.dot_general(placing, zbuf[origin(s)], (((0,), (0,)), ((), ())), preferred_element_type=F32)
         xs[s] = packed.astype(BF16).reshape(inner, cap, wide)
         for d in range(1, inner):
             x_copy(s, d).start()
@@ -142,9 +170,10 @@
         f_copy(s, 0).start()
 
     def compute(s):
-        rows = xr[s].reshape(2 * group, wide)
-        gate_act = jnp.dot(rows, gate_w[...], preferred_element_type=F32)
-        up_act = jnp.dot(rows, up_w[...], preferred_element_type=F32)
+        rows = xr[s, :, :, :, :width].reshape(2 * group, width)
+        across = (((1,), (1,)), ((), ()))
+        gate_act = lax.dot_general(rows, gate_w[...], across, preferred_element_type=F32)
+        up_act = lax.dot_general(rows, up_w[...], across, preferred_element_type=F32)
         hidden = (gate_act * jax.nn.sigmoid(1.702 * gate_act) * (up_act + 1.0)).astype(BF16)
         part[s % 2] = jnp.dot(hidden, down_w[...], preferred_element_type=F32).reshape(2, group, width)
         tbuf[s] = part[s % 2, other].astype(BF16)
@@ -171,17 +200,34 @@
         both = jnp.dot(mixing, yrecv[s].reshape(group, width), preferred_element_type=F32)
         return both[:tok_count] + both[tok_count:]
 
-    for s in range(1, outer):
-        z_copy(s).start()
+    @pl.when(z + 1 < outer)
+    def _():
+        z_copy(z, 1).start()
+
+    @pl.when(z > 0)
+    def _():
+        z_copy(z, 0).start()
+
     dispatch(0)
-    for load in loads:
-        load.wait()
 
     def step(i, carry):
         @pl.when(i + 1 < outer)
         def _():
-            z_copy(i + 1).wait_recv()
+            pass_on(i + 1)
             dispatch(i + 1)
+
+        @pl.when((i >= 1) & (i <= outer))
+        def _():
+            give_back(i - 1)
+
+        @pl.when(i == 2)
+        def _():
+            acc[...] = combine(0)
+
+        @pl.when(i > 2)
+        def _():
+            cbuf[i - 2] = combine(i - 2).astype(BF16)
+            c_copy(i - 2, origin(i - 2)).start()
 
         @pl.when(i < outer)
         def _():
@@ -190,20 +236,15 @@
                 f_copy(i, d).start()
             for d in range(inner):
                 f_copy(i, d, True).wait_recv()
+
+        @pl.when(i == 0)
+        def _():
+            for load in loads:
+                load.wait()
+
+        @pl.when(i < outer)
+        def _():
             compute(i)
-
-        @pl.when((i >= 1) & (i <= outer))
-        def _():
-            give_back(i - 1)
-
-        @pl.when(i == 2)
-        def _():
-            acc[...] = combine(0)
-
-        @pl.when(i > 2)
-        def _():
-            cbuf[i - 2] = combine(i - 2).astype(BF16)
-            c_copy(i - 2).start()
 
         return carry
 
@@ -211,8 +252,9 @@
 
     total = acc[...]
     for s in range(1, outer):
-        c_copy(s).wait_recv()
-        total = total + crecv[s].astype(F32)
+        peer = (z + s) % outer
+        c_copy(s, peer, True).wait_recv()
+        total = total + crecv[peer].astype(F32)
     out_ref[...] = total.astype(BF16)
 
     for s in range(outer):
@@ -223,8 +265,15 @@
             f_copy(s, d).wait_send()
         t_copy(s).wait_send()
         if s > 0:
-            z_copy(s).wait_send()
-            c_copy(s).wait_send()
+            c_copy(s, origin(s)).wait_send()
+
+        @pl.when((s <= z) & (z + 1 < outer))
+        def _():
+            z_copy(s, 1).wait_send()
+
+        @pl.when((s >= z) & (z > 0))
+        def _():
+            z_copy(s, 0).wait_send()
 
 
 def split_of(experts):
@@ -246,8 +295,7 @@
     if cap % 16 or tok_dev % 16 or tok_dev > 256 or width % 16 or half % 16:
         return None
     rows = outer * inner * cap
-    lanes = -(-half // 128) * 128
-    held = 2 * wide * (2 * lanes + half + 7 * rows + 3 * outer * tok_dev) + 16 * wide * inner * cap
+    held = 2 * wide * (3 * half + 7 * rows + 3 * outer * tok_dev) + 16 * wide * inner * cap
     if held > 44 * 2**20:
         return None
     return outer, inner, cap, picks, width, wide
@@ -258,7 +306,7 @@
     tok_dev = tokens.shape[0]
     half = gate_weight.shape[2]
     group = inner * cap
-    padded = jnp.pad(tokens, ((0, 0), (0, wide - width)))
+    gate, up = gate_weight.swapaxes(1, 2), up_weight.swapaxes(1, 2)
     vmem, hbm = pl.BlockSpec(memory_space=pltpu.VMEM), pl.BlockSpec(memory_space=pl.ANY)
     dma = pltpu.SemaphoreType.DMA
     rows = 2 * outer * group
@@ -271,8 +319,8 @@
             pltpu.VMEM((outer, tok_dev, wide), BF16),
             pltpu.VMEM((outer, inner, cap, wide), BF16),
             pltpu.VMEM((outer, 2, inner, cap, wide), BF16),
-            pltpu.VMEM((wide, half), BF16),
-            pltpu.VMEM((wide, half), BF16),
+            pltpu.VMEM((half, width), BF16),
+            pltpu.VMEM((half, width), BF16),
             pltpu.VMEM((half, width), BF16),
             pltpu.VMEM((2, 2, group, width), F32),
             pltpu.VMEM((outer, group, width), BF16),
@@ -283,7 +331,7 @@
             pltpu.VMEM((outer, tok_dev, width), BF16),
             pltpu.VMEM((tok_dev, width), F32),
             dma((3,)),
-            dma((outer,)), dma((outer,)),
+            dma((2, outer)), dma((outer,)),
             dma((outer, inner)), dma((outer, inner)),
             dma((outer, inner)), dma((outer, inner)),
             dma((outer,)), dma((outer,)),
@@ -296,7 +344,7 @@
         cost_estimate=pl.CostEstimate(
             flops=6 * rows * width * half, bytes_accessed=6 * width * half, transcendentals=rows * half
         ),
-    )(padded, expert_ids, route_logits, gate_weight, up_weight, down_weight)
+    )(tokens, expert_ids.T, route_logits.T, gate, up, down_weight)
 
 
 def plain(tokens, expert_ids, route_logits, gate_weight, up_weight, down_weight):

time: 80.1 us -> 65.7 us (0.82)
  the two profiles are of different devices: /device:TPU:8 before, /device:TPU:0 now
where the time goes in v2:
time: 65.7 us; the launch traced here: 65.5 us
  Pallas kernels  63.9 us (97%)
  local copies, waits for them, and re-layouts  1.61 us (2%)
    pallas_call x1, Pallas kernels, fused(): pl.pallas_call(functools.partial(moe_kernel, sizes), out_shape=jax.ShapeD...  63.9 us
    unnamed x1, local copies, waits for them, and re-layouts  1.61 us

profile of v2, /device:TPU:0, one launch (start us, length us, event | category | flops | bytes accessed | tf_op | source)
XLA Modules:
  0.0 65.5 jit_solution(8210332151306501819)
XLA Ops:
  0.0 63.9 %shard_map.64 = bf16[32,2880]{1,0:T(8,128)(2,1)} custom-call(bf16[32,2880]{1,0:T(8,128)(2,1)} %tok_ref.1, s32[4,32]{1,0:T(4,128)} %bitcast.6, f32[4,32]{1,0:T(4,128)} %bitcast.7, bf16[1,720,2880]{2,1,0:T(8,128)(2,1)} %bitcast.4, bf16[1,720,2880]{2,1,0:T(8,128)(2,1)} %bitcast.5, bf16[1,720,2880]{2,1,0:T(8,128)(2,1)} %down_hbm.1), custom_call_target="tpu_custom_call" | custom-call | flops 6370099200 | bytes 12441600 | tf_op jit(solution)/shard_map/pallas_call | solution.py:313
  63.9 1.6 %copy.8 = bf16[32,2880]{1,0:T(8,128)(2,1)} copy(bf16[32,2880]{1,0:T(8,128)(2,1)} %shard_map.64) | data formatting | bytes 368640

commit v3 on v2

--- a/solution.py
+++ b/solution.py
@@ -24,9 +24,9 @@
     sizes,
     tok_ref, ids_ref, logit_ref, gate_hbm, up_hbm, down_hbm,
     out_ref,
-    zbuf, xs, xr, gate_w, up_w, down_w, part, tbuf, trecv, ybuf, yrecv, cbuf, crecv, acc,
+    zbuf, xs, xr, gate_w, up_w, down_w, part, tbuf, trecv, ybuf, yrecv, cbuf, crecv, acc, held, handed,
     wsem, zsend_sem, zrecv_sem, xsend_sem, xrecv_sem, fsend_sem, frecv_sem,
-    tsend_sem, trecv_sem, ysend_sem, yrecv_sem, csend_sem, crecv_sem,
+    tsend_sem, trecv_sem, ysend_sem, yrecv_sem, csend_sem, crecv_sem, hand_sem,
 ):
     outer, inner, cap, picks, width, wide = sizes
     tok_count = tok_ref.shape[0]
@@ -147,6 +147,21 @@
             device_id=(peer * inner + p, c), device_id_type=MESH,
         )
 
+    mate = z + 1 - 2 * (z % 2)
+
+    def hand_copy(s, block):
+        return pltpu.make_async_remote_copy(
+            src_ref=cbuf.at[s], dst_ref=handed.at[block],
+            send_sem=csend_sem.at[s], recv_sem=hand_sem.at[block],
+            device_id=(mate * inner + p, c), device_id_type=MESH,
+        )
+
+    def role(s):
+        block = origin(s)
+        within = block // 2 == z // 2
+        nearer = jnp.where(block > z, z % 2 == 1, z % 2 == 0)
+        return block, within, nearer
+
     def notes(s):
         told = zbuf[origin(s), :, wide - 128 :].astype(F32)
         found = []
@@ -226,8 +241,19 @@
 
         @pl.when(i > 2)
         def _():
-            cbuf[i - 2] = combine(i - 2).astype(BF16)
-            c_copy(i - 2, origin(i - 2)).start()
+            s = i - 2
+            block, within, nearer = role(s)
+            held[s] = combine(s)
+
+            @pl.when(within)
+            def _():
+                cbuf[s] = held[s].astype(BF16)
+                c_copy(s, block).start()
+
+            @pl.when(jnp.logical_not(within) & jnp.logical_not(nearer))
+            def _():
+                cbuf[s] = held[s].astype(BF16)
+                hand_copy(s, block).start()
 
         @pl.when(i < outer)
         def _():
@@ -250,10 +276,21 @@
 
     lax.fori_loop(0, outer + 2, step, 0)
 
+    for s in range(1, outer):
+        block, within, nearer = role(s)
+
+        @pl.when(jnp.logical_not(within) & nearer)
+        def _():
+            hand_copy(s, block).wait_recv()
+            cbuf[s] = (held[s] + handed[block].astype(F32)).astype(BF16)
+            c_copy(s, block).start()
+
     total = acc[...]
-    for s in range(1, outer):
-        peer = (z + s) % outer
-        c_copy(s, peer, True).wait_recv()
+    pairs = outer // 2
+    for r in range(pairs):
+        pair = (z // 2 + r) % pairs
+        peer = mate if r == 0 else jnp.where(2 * pair > z, 2 * pair, 2 * pair + 1)
+        c_copy(1, peer, True).wait_recv()
         total = total + crecv[peer].astype(F32)
     out_ref[...] = total.astype(BF16)
 
@@ -295,7 +332,7 @@
     if cap % 16 or tok_dev % 16 or tok_dev > 256 or width % 16 or half % 16:
         return None
     rows = outer * inner * cap
-    held = 2 * wide * (3 * half + 7 * rows + 3 * outer * tok_dev) + 16 * wide * inner * cap
+    held = 2 * wide * (3 * half + 7 * rows + 6 * outer * tok_dev) + 16 * wide * inner * cap
     if held > 44 * 2**20:
         return None
     return outer, inner, cap, picks, width, wide
@@ -330,13 +367,15 @@
             pltpu.VMEM((outer, tok_dev, width), BF16),
             pltpu.VMEM((outer, tok_dev, width), BF16),
             pltpu.VMEM((tok_dev, width), F32),
+            pltpu.VMEM((outer, tok_dev, width), F32),
+            pltpu.VMEM((outer, tok_dev, width), BF16),
             dma((3,)),
             dma((2, outer)), dma((outer,)),
             dma((outer, inner)), dma((outer, inner)),
             dma((outer, inner)), dma((outer, inner)),
             dma((outer,)), dma((outer,)),
             dma((outer, inner)), dma((outer, inner)),
-            dma((outer,)), dma((outer,)),
+            dma((outer,)), dma((outer,)), dma((outer,)),
         ],
         compiler_params=pltpu.CompilerParams(
             collective_id=0, has_side_effects=True, vmem_limit_bytes=56 * 2**20

time: 65.7 us -> 63.7 us (0.970)
  Pallas kernels: 63.9 us -> 61.9 us
    pallas_call x1, Pallas kernels: 63.9 us -> 61.9 us  [fused(): pl.pallas_call(functools.partial(moe_kernel, sizes), out_shape=jax.ShapeD...]
where the time goes in v3:
time: 63.7 us; the launch traced here: 63.5 us
  Pallas kernels  61.9 us (97%)
  local copies, waits for them, and re-layouts  1.61 us (3%)
    pallas_call x1, Pallas kernels, fused(): pl.pallas_call(functools.partial(moe_kernel, sizes), out_shape=jax.ShapeD...  61.9 us
    unnamed x1, local copies, waits for them, and re-layouts  1.61 us

profile of v3, /device:TPU:0, one launch (start us, length us, event | category | flops | bytes accessed | tf_op | source)
XLA Modules:
  0.0 63.5 jit_solution(8302683939415552408)
XLA Ops:
  0.0 61.9 %shard_map.64 = bf16[32,2880]{1,0:T(8,128)(2,1)} custom-call(bf16[32,2880]{1,0:T(8,128)(2,1)} %tok_ref.1, s32[4,32]{1,0:T(4,128)} %bitcast.6, f32[4,32]{1,0:T(4,128)} %bitcast.7, bf16[1,720,2880]{2,1,0:T(8,128)(2,1)} %bitcast.4, bf16[1,720,2880]{2,1,0:T(8,128)(2,1)} %bitcast.5, bf16[1,720,2880]{2,1,0:T(8,128)(2,1)} %down_hbm.1), custom_call_target="tpu_custom_call" | custom-call | flops 6370099200 | bytes 12441600 | tf_op jit(solution)/shard_map/pallas_call | solution.py:350
  61.9 1.6 %copy.8 = bf16[32,2880]{1,0:T(8,128)(2,1)} copy(bf16[32,2880]{1,0:T(8,128)(2,1)} %shard_map.64) | data formatting | bytes 368640

commit v4 on v3

--- a/solution.py
+++ b/solution.py
@@ -24,7 +24,7 @@
     sizes,
     tok_ref, ids_ref, logit_ref, gate_hbm, up_hbm, down_hbm,
     out_ref,
-    zbuf, xs, xr, gate_w, up_w, down_w, part, tbuf, trecv, ybuf, yrecv, cbuf, crecv, acc, held, handed,
+    zbuf, xs, xr, gate_w, up_w, down_w, part, tbuf, trecv, ybuf, yrecv, cbuf, crecv, held, handed,
     wsem, zsend_sem, zrecv_sem, xsend_sem, xrecv_sem, fsend_sem, frecv_sem,
     tsend_sem, trecv_sem, ysend_sem, yrecv_sem, csend_sem, crecv_sem, hand_sem,
 ):
@@ -82,9 +82,10 @@
     def origin(s):
         near = jnp.minimum(z, outer - 1 - z)
         toward = jnp.where(2 * z < outer, -1, 1)
-        j = (s + 1) // 2
-        paired = jnp.where(s % 2 == 1, toward * j, -toward * j)
-        return z + jnp.where(s <= 2 * near, paired, -toward * (s - near))
+        turn = (s + 1) % outer
+        j = (turn + 1) // 2
+        paired = jnp.where(turn % 2 == 1, toward * j, -toward * j)
+        return z + jnp.where(turn <= 2 * near, paired, -toward * (turn - near))
 
     def z_copy(block, way):
         return pltpu.make_async_remote_copy(
@@ -223,23 +224,22 @@
     def _():
         z_copy(z, 0).start()
 
-    dispatch(0)
+    dispatch(outer - 1)
+    if outer > 1:
+        pass_on(1)
+        dispatch(0)
 
     def step(i, carry):
-        @pl.when(i + 1 < outer)
-        def _():
-            pass_on(i + 1)
+        @pl.when(i + 2 < outer)
+        def _():
+            pass_on(i + 2)
             dispatch(i + 1)
 
         @pl.when((i >= 1) & (i <= outer))
         def _():
             give_back(i - 1)
 
-        @pl.when(i == 2)
-        def _():
-            acc[...] = combine(0)
-
-        @pl.when(i > 2)
+        @pl.when((i >= 2) & (i <= outer))
         def _():
             s = i - 2
             block, within, nearer = role(s)
@@ -274,9 +274,9 @@
 
         return carry
 
-    lax.fori_loop(0, outer + 2, step, 0)
-
-    for s in range(1, outer):
+    lax.fori_loop(0, outer + 1, step, 0)
+
+    for s in range(outer - 1):
         block, within, nearer = role(s)
 
         @pl.when(jnp.logical_not(within) & nearer)
@@ -285,12 +285,12 @@
             cbuf[s] = (held[s] + handed[block].astype(F32)).astype(BF16)
             c_copy(s, block).start()
 
-    total = acc[...]
+    total = combine(outer - 1)
     pairs = outer // 2
     for r in range(pairs):
         pair = (z // 2 + r) % pairs
         peer = mate if r == 0 else jnp.where(2 * pair > z, 2 * pair, 2 * pair + 1)
-        c_copy(1, peer, True).wait_recv()
+        c_copy(0, peer, True).wait_recv()
         total = total + crecv[peer].astype(F32)
     out_ref[...] = total.astype(BF16)
 
@@ -301,7 +301,7 @@
         for d in range(inner):
             f_copy(s, d).wait_send()
         t_copy(s).wait_send()
-        if s > 0:
+        if s < outer - 1:
             c_copy(s, origin(s)).wait_send()
 
         @pl.when((s <= z) & (z + 1 < outer))
@@ -366,7 +366,6 @@
             pltpu.VMEM((outer, inner, cap, width), BF16),
             pltpu.VMEM((outer, tok_dev, width), BF16),
             pltpu.VMEM((outer, tok_dev, width), BF16),
-            pltpu.VMEM((tok_dev, width), F32),
             pltpu.VMEM((outer, tok_dev, width), F32),
             pltpu.VMEM((outer, tok_dev, width), BF16),
             dma((3,)),

time: 63.7 us -> 62.6 us (0.983)
  Pallas kernels: 61.9 us -> 60.8 us
    pallas_call x1, Pallas kernels: 61.9 us -> 60.8 us  [fused(): pl.pallas_call(functools.partial(moe_kernel, sizes), out_shape=jax.ShapeD...]
where the time goes in v4:
time: 62.6 us; the launch traced here: 62.4 us
  Pallas kernels  60.8 us (97%)
  local copies, waits for them, and re-layouts  1.61 us (3%)
    pallas_call x1, Pallas kernels, fused(): pl.pallas_call(functools.partial(moe_kernel, sizes), out_shape=jax.ShapeD...  60.8 us
    unnamed x1, local copies, waits for them, and re-layouts  1.61 us

profile of v4, /device:TPU:0, one launch (start us, length us, event | category | flops | bytes accessed | tf_op | source)
XLA Modules:
  0.0 62.4 jit_solution(18065156203188584476)
XLA Ops:
  0.0 60.8 %shard_map.64 = bf16[32,2880]{1,0:T(8,128)(2,1)} custom-call(bf16[32,2880]{1,0:T(8,128)(2,1)} %tok_ref.1, s32[4,32]{1,0:T(4,128)} %bitcast.6, f32[4,32]{1,0:T(4,128)} %bitcast.7, bf16[1,720,2880]{2,1,0:T(8,128)(2,1)} %bitcast.4, bf16[1,720,2880]{2,1,0:T(8,128)(2,1)} %bitcast.5, bf16[1,720,2880]{2,1,0:T(8,128)(2,1)} %down_hbm.1), custom_call_target="tpu_custom_call" | custom-call | flops 6370099200 | bytes 12441600 | tf_op jit(solution)/shard_map/pallas_call | solution.py:350
  60.8 1.6 %copy.8 = bf16[32,2880]{1,0:T(8,128)(2,1)} copy(bf16[32,2880]{1,0:T(8,128)(2,1)} %shard_map.64) | data formatting | bytes 368640
